TPU v7x, 32 devices: a whole 2x2x4 slice. The times are simulated.
32 devices in a mesh: row: 4 (over z), col: 8 (over y, x, core).
Axes of the slice: x: 2, y: 2, z: 4, core: 2. Of those that a mesh axis runs over, the one named last changes fastest.
Arguments:
- inputs: bfloat16 [4096, 2048], P('row', 'col'), may hold values from -6 to 6
- query_weight: bfloat16 [2048, 2048], P('row', 'col'), may hold values from -0.125 to 0.125
- key_weight: bfloat16 [2048, 2048], P('row', 'col'), may hold values from -0.125 to 0.125
- value_weight: bfloat16 [2048, 2048], P('row', 'col'), may hold values from -0.125 to 0.125
- out_weight: bfloat16 [2048, 2048], P('row', 'col'), may hold values from -2 to 2
- gate_weight: bfloat16 [2048, 8192], P('row', 'col'), may hold values from -0.125 to 0.125
- up_weight: bfloat16 [2048, 8192], P('row', 'col'), may hold values from -0.125 to 0.125
- down_weight: bfloat16 [2048, 8192], P('row', 'col'), may hold values from -0.0625 to 0.0625
- first_gain: bfloat16 [2048], P('row'), may hold values from 0.5 to 1.5
- second_gain: bfloat16 [2048], P('row'), may hold values from 0.5 to 1.5
- segment_ids: int32 [4096], P('row'), may hold values from 0 to 7, as said below
- positions: int32 [4096], P('row'), may hold values from 0 to 767, as said below
- out_grad: bfloat16 [4096, 2048], P('row', 'col'), may hold values from -6 to 6
Outputs:
- block_out: bfloat16 [4096, 2048], P('row', 'col')
- input_grad: bfloat16 [4096, 2048], P('row', 'col')
- query_weight_grad: float32 [2048, 2048], P('row', 'col')
- key_weight_grad: float32 [2048, 2048], P('row', 'col')
- value_weight_grad: float32 [2048, 2048], P('row', 'col')
- out_weight_grad: float32 [2048, 2048], P('row', 'col')
- gate_weight_grad: float32 [2048, 8192], P('row', 'col')
- up_weight_grad: float32 [2048, 8192], P('row', 'col')
- down_weight_grad: float32 [2048, 8192], P('row', 'col')
- first_gain_grad: float32 [2048], P('row')
- second_gain_grad: float32 [2048], P('row')
Inputs may be any that keep to these rules, and one draw needn't show every extreme that they name: `segment_ids`: ids never fall along the rows. Each aligned block of 1024 rows holds two documents, numbered 2 b and 2 b + 1 in block b; the second starts at a row from 256 to 768 of its block. `positions`: each row's offset from the first row of its document.
All inputs are finite; a program needn't handle non-finite values.
Results may differ from a plain program's by a relative error of at most 0.019.
Values may be sent and summed in bfloat16 or wider, within the bound.
No kernel may reach another device: no remote copies, remote signals or barrier semaphores. Data moves between devices by JAX's collectives and lax.ppermute only.
A program may use at most 192 MiB of HBM per device.

v0:
```python
import math
import jax
import jax.numpy as jnp
from jax import lax
from jax.sharding import PartitionSpec as P

HEAD_DIM = 64
SEQ = 1024
eps = 1e-05
rope_base = 130000.0


def rope_tables(positions, head_size):
    half_size = head_size // 2
    freqs = jnp.exp(
        jnp.arange(half_size, dtype=jnp.float32) * (-2.0 * math.log(rope_base) / head_size)
    )
    angles = positions.astype(jnp.float32)[:, None] * freqs[None, :]
    return (jnp.cos(angles), jnp.sin(angles))


def rotate(values, cosine, sine):
    half_size = values.shape[-1] // 2
    front_half = values[..., :half_size]
    back_half = values[..., half_size:]
    cosine_wide = cosine[:, None, :]
    sine_wide = sine[:, None, :]
    return jnp.concatenate(
        [
            front_half * cosine_wide - back_half * sine_wide,
            back_half * cosine_wide + front_half * sine_wide,
        ],
        axis=-1,
    )


def unrotate(values, cosine, sine):
    half_size = values.shape[-1] // 2
    front_half = values[..., :half_size]
    back_half = values[..., half_size:]
    cosine_wide = cosine[:, None, :]
    sine_wide = sine[:, None, :]
    return jnp.concatenate(
        [
            front_half * cosine_wide + back_half * sine_wide,
            back_half * cosine_wide - front_half * sine_wide,
        ],
        axis=-1,
    )


def contract_last(left, right):
    return lax.dot_general(
        left, right, (((1,), (1,)), ((), ())), preferred_element_type=jnp.float32
    )


def contract_first(left, right):
    return lax.dot_general(
        left, right, (((0,), (0,)), ((), ())), preferred_element_type=jnp.float32
    )


def block_mask(segment_ids, row_start, seq_start, block_rows):
    query_ids = lax.dynamic_slice_in_dim(segment_ids, row_start, block_rows, 0)
    query_index = row_start + jnp.arange(block_rows)
    key_index = seq_start + jnp.arange(SEQ)
    return (query_ids[:, None] == segment_ids[None, :]) & (
        query_index[:, None] >= key_index[None, :]
    )


def block_scores(query_piece, key_piece, allowed):
    scores = jnp.einsum(
        "qhd,khd->hqk", query_piece, key_piece, preferred_element_type=jnp.float32
    ) * HEAD_DIM ** (-0.5)
    return jnp.where(allowed[None], scores, -1e30)


def attend_forward(query_rows, key_rows, value_rows, segment_ids):
    token_count, heads_here, head_size = query_rows.shape
    block_rows = min(512, SEQ)
    block_count = token_count // block_rows

    def one_block(index_block):
        row_start = index_block * block_rows
        seq_start = row_start // SEQ * SEQ
        query_piece = lax.dynamic_slice_in_dim(query_rows, row_start, block_rows, 0)
        scores = block_scores(
            query_piece, key_rows, block_mask(segment_ids, row_start, seq_start, block_rows)
        )
        peak = jnp.max(scores, axis=-1, keepdims=True)
        raised = jnp.exp(scores - peak)
        denominator = jnp.sum(raised, axis=-1, keepdims=True)
        weights = (raised / denominator).astype(jnp.bfloat16)
        attended = jnp.einsum(
            "hqk,khd->qhd", weights, value_rows, preferred_element_type=jnp.float32
        )
        return (attended.astype(jnp.bfloat16), (peak + jnp.log(denominator))[..., 0])

    attended, logsum = lax.map(one_block, jnp.arange(block_count))
    return (attended.reshape(token_count, heads_here * head_size), logsum)


def attend_backward(query_rows, key_rows, value_rows, mixed_grad, logsum, segment_ids):
    token_count, heads_here, head_size = query_rows.shape
    block_rows = min(512, SEQ)
    block_count = token_count // block_rows
    score_scale = HEAD_DIM ** (-0.5)

    def one_block(carry, pieces):
        key_grad, value_grad = carry
        index_block, logsum_piece = pieces
        row_start = index_block * block_rows
        seq_start = row_start // SEQ * SEQ
        query_piece = lax.dynamic_slice_in_dim(query_rows, row_start, block_rows, 0)
        grad_piece = lax.dynamic_slice_in_dim(mixed_grad, row_start, block_rows, 0)
        scores = block_scores(
            query_piece, key_rows, block_mask(segment_ids, row_start, seq_start, block_rows)
        )
        weights = jnp.exp(scores - logsum_piece[..., None])
        weight_grad = jnp.einsum(
            "qhd,khd->hqk", grad_piece, value_rows, preferred_element_type=jnp.float32
        )
        row_dots = jnp.sum(weights * weight_grad, axis=-1, keepdims=True)
        score_grad = (weights * (weight_grad - row_dots)).astype(jnp.bfloat16)
        query_grad = (
            jnp.einsum("hqk,khd->qhd", score_grad, key_rows, preferred_element_type=jnp.float32)
            * score_scale
        )
        key_add = (
            jnp.einsum("hqk,qhd->khd", score_grad, query_piece, preferred_element_type=jnp.float32)
            * score_scale
        )
        value_add = jnp.einsum(
            "hqk,qhd->khd",
            weights.astype(jnp.bfloat16),
            grad_piece,
            preferred_element_type=jnp.float32,
        )
        key_grad = key_grad + key_add
        value_grad = value_grad + value_add
        return ((key_grad, value_grad), query_grad)

    zeros_grad = jnp.zeros((token_count, heads_here, head_size), jnp.float32)
    (key_grad, value_grad), query_grad = lax.scan(
        one_block, (zeros_grad, zeros_grad), (jnp.arange(block_count), logsum)
    )
    return (query_grad.reshape(token_count, heads_here, head_size), key_grad, value_grad)


def local(
    inputs,
    query_weight,
    key_weight,
    value_weight,
    out_weight,
    gate_weight,
    up_weight,
    down_weight,
    first_gain,
    second_gain,
    segment_ids,
    positions,
    out_grad,
):
    col_index = lax.axis_index("col")
    feat_here = inputs.shape[1]
    width = feat_here * lax.axis_size("col")
    token_count = inputs.shape[0]
    heads_here = query_weight.shape[1] // HEAD_DIM
    gathered = (
        lax.all_gather(query_weight, "row", axis=0, tiled=True),
        lax.all_gather(key_weight, "row", axis=0, tiled=True),
        lax.all_gather(value_weight, "row", axis=0, tiled=True),
        lax.all_gather(out_weight, "row", axis=0, tiled=True),
        lax.all_gather(gate_weight, "row", axis=0, tiled=True),
        lax.all_gather(up_weight, "row", axis=0, tiled=True),
        lax.all_gather(down_weight, "row", axis=0, tiled=True),
        lax.all_gather(first_gain, "row", axis=0, tiled=True),
        lax.all_gather(second_gain, "row", axis=0, tiled=True),
    )
    (
        query_full,
        key_full,
        value_full,
        out_full,
        gate_full,
        up_full,
        down_full,
        gain_one,
        gain_two,
    ) = gathered
    gain_one = gain_one.astype(jnp.float32)
    gain_two = gain_two.astype(jnp.float32)
    gain_one_block = lax.dynamic_slice_in_dim(gain_one, col_index * feat_here, feat_here, 0)
    gain_two_block = lax.dynamic_slice_in_dim(gain_two, col_index * feat_here, feat_here, 0)
    input_rows = lax.all_gather(inputs, "col", axis=1, tiled=True).astype(jnp.float32)
    scale_one = lax.rsqrt(jnp.mean(input_rows * input_rows, axis=1, keepdims=True) + eps)
    unit_one = input_rows * scale_one
    normed_one = (unit_one * gain_one).astype(jnp.bfloat16)
    cosine, sine = rope_tables(positions, HEAD_DIM)
    query_pre = jnp.dot(normed_one, query_full, preferred_element_type=jnp.float32).reshape(
        token_count, heads_here, HEAD_DIM
    )
    key_pre = jnp.dot(normed_one, key_full, preferred_element_type=jnp.float32).reshape(
        token_count, heads_here, HEAD_DIM
    )
    query_rows = rotate(query_pre, cosine, sine).astype(jnp.bfloat16)
    key_rows = rotate(key_pre, cosine, sine).astype(jnp.bfloat16)
    value_rows = (
        jnp.dot(normed_one, value_full, preferred_element_type=jnp.float32)
        .astype(jnp.bfloat16)
        .reshape(token_count, heads_here, HEAD_DIM)
    )
    mixed, logsum = attend_forward(query_rows, key_rows, value_rows, segment_ids)
    input_block = inputs.astype(jnp.float32)
    attention_part = contract_last(mixed, out_full)
    attention_block = lax.psum_scatter(attention_part, "col", scatter_dimension=1, tiled=True)
    middle_block = input_block + attention_block
    middle_rows = lax.all_gather(middle_block, "col", axis=1, tiled=True)
    scale_two = lax.rsqrt(jnp.mean(middle_rows * middle_rows, axis=1, keepdims=True) + eps)
    unit_two = middle_rows * scale_two
    normed_two = (unit_two * gain_two).astype(jnp.bfloat16)
    gate_rows = jnp.dot(normed_two, gate_full, preferred_element_type=jnp.float32)
    up_rows = jnp.dot(normed_two, up_full, preferred_element_type=jnp.float32)
    sigmoid_gate = jax.nn.sigmoid(gate_rows)
    silu_gate = gate_rows * sigmoid_gate
    hidden = (silu_gate * up_rows).astype(jnp.bfloat16)
    feed_part = contract_last(hidden, down_full)
    feed_block = lax.psum_scatter(
        feed_part.astype(jnp.bfloat16), "col", scatter_dimension=1, tiled=True
    ).astype(jnp.float32)
    block_out = (middle_block + feed_block).astype(jnp.bfloat16)
    grad_rows = lax.all_gather(out_grad, "col", axis=1, tiled=True)
    hidden_grad = jnp.dot(grad_rows, down_full, preferred_element_type=jnp.float32)
    down_weight_grad = contract_first(grad_rows, hidden)
    gate_grad = (
        hidden_grad * up_rows * sigmoid_gate * (1.0 + gate_rows * (1.0 - sigmoid_gate))
    ).astype(jnp.bfloat16)
    up_grad = (hidden_grad * silu_gate).astype(jnp.bfloat16)
    gate_weight_grad = contract_first(normed_two, gate_grad)
    up_weight_grad = contract_first(normed_two, up_grad)
    normed_two_grad = contract_last(gate_grad, gate_full) + contract_last(up_grad, up_full)
    gain_two_part = jnp.sum(normed_two_grad * unit_two, axis=0)
    token_two_part = jnp.sum(normed_two_grad * gain_two * unit_two, axis=1)
    token_two, gain_two_grad = lax.psum((token_two_part, gain_two_part), "col")
    normed_two_block = lax.psum_scatter(
        normed_two_grad.astype(jnp.bfloat16), "col", scatter_dimension=1, tiled=True
    ).astype(jnp.float32)
    unit_two_block = lax.dynamic_slice_in_dim(unit_two, col_index * feat_here, feat_here, 1)
    middle_grad = out_grad.astype(jnp.float32) + scale_two * (
        normed_two_block * gain_two_block - unit_two_block * (token_two[:, None] / width)
    )
    middle_rows_grad = lax.all_gather(middle_grad.astype(jnp.bfloat16), "col", axis=1, tiled=True)
    mixed_grad = jnp.dot(middle_rows_grad, out_full, preferred_element_type=jnp.float32).astype(
        jnp.bfloat16
    )
    out_weight_grad = contract_first(middle_rows_grad, mixed)
    query_grad, key_grad, value_grad = attend_backward(
        query_rows,
        key_rows,
        value_rows,
        mixed_grad.reshape(token_count, heads_here, HEAD_DIM),
        logsum,
        segment_ids,
    )
    query_grad = (
        unrotate(query_grad, cosine, sine)
        .astype(jnp.bfloat16)
        .reshape(token_count, heads_here * HEAD_DIM)
    )
    key_grad = (
        unrotate(key_grad, cosine, sine)
        .astype(jnp.bfloat16)
        .reshape(token_count, heads_here * HEAD_DIM)
    )
    value_grad = value_grad.astype(jnp.bfloat16).reshape(token_count, heads_here * HEAD_DIM)
    query_weight_grad = contract_first(normed_one, query_grad)
    key_weight_grad = contract_first(normed_one, key_grad)
    value_weight_grad = contract_first(normed_one, value_grad)
    normed_one_grad = (
        contract_last(query_grad, query_full)
        + contract_last(key_grad, key_full)
        + contract_last(value_grad, value_full)
    )
    gain_one_part = jnp.sum(normed_one_grad * unit_one, axis=0)
    token_one_part = jnp.sum(normed_one_grad * gain_one * unit_one, axis=1)
    token_one, gain_one_grad = lax.psum((token_one_part, gain_one_part), "col")
    normed_one_block = lax.psum_scatter(
        normed_one_grad.astype(jnp.bfloat16), "col", scatter_dimension=1, tiled=True
    ).astype(jnp.float32)
    unit_one_block = lax.dynamic_slice_in_dim(unit_one, col_index * feat_here, feat_here, 1)
    input_grad = (
        middle_grad
        + scale_one
        * (normed_one_block * gain_one_block - unit_one_block * (token_one[:, None] / width))
    ).astype(jnp.bfloat16)
    summed = (
        lax.psum_scatter(
            query_weight_grad.astype(jnp.bfloat16), "row", scatter_dimension=0, tiled=True
        ).astype(jnp.float32),
        lax.psum_scatter(
            key_weight_grad.astype(jnp.bfloat16), "row", scatter_dimension=0, tiled=True
        ).astype(jnp.float32),
        lax.psum_scatter(
            value_weight_grad.astype(jnp.bfloat16), "row", scatter_dimension=0, tiled=True
        ).astype(jnp.float32),
        lax.psum_scatter(
            out_weight_grad.astype(jnp.bfloat16), "row", scatter_dimension=0, tiled=True
        ).astype(jnp.float32),
        lax.psum_scatter(
            gate_weight_grad.astype(jnp.bfloat16), "row", scatter_dimension=0, tiled=True
        ).astype(jnp.float32),
        lax.psum_scatter(
            up_weight_grad.astype(jnp.bfloat16), "row", scatter_dimension=0, tiled=True
        ).astype(jnp.float32),
        lax.psum_scatter(
            down_weight_grad.astype(jnp.bfloat16), "row", scatter_dimension=0, tiled=True
        ).astype(jnp.float32),
        lax.psum_scatter(
            gain_one_grad.astype(jnp.bfloat16), "row", scatter_dimension=0, tiled=True
        ).astype(jnp.float32),
        lax.psum_scatter(
            gain_two_grad.astype(jnp.bfloat16), "row", scatter_dimension=0, tiled=True
        ).astype(jnp.float32),
    )
    return (block_out, input_grad) + tuple(summed)


def solution(mesh):
    return jax.shard_map(
        local,
        mesh=mesh,
        in_specs=(
            P("row", "col"),
            P("row", "col"),
            P("row", "col"),
            P("row", "col"),
            P("row", "col"),
            P("row", "col"),
            P("row", "col"),
            P("row", "col"),
            P("row"),
            P("row"),
            P("row"),
            P("row"),
            P("row", "col"),
        ),
        out_specs=(
            P("row", "col"),
            P("row", "col"),
            P("row", "col"),
            P("row", "col"),
            P("row", "col"),
            P("row", "col"),
            P("row", "col"),
            P("row", "col"),
            P("row", "col"),
            P("row"),
            P("row"),
        ),
        check_vma=False,
    )
```

profile of v0, /device:TPU:0, one launch (start us, length us, event | category | flops | bytes accessed | tf_op | source)
XLA Modules:
  0.0 1178.5 jit_solution(17229201245399395030)
XLA Ops:
  12.0 13.5 %all-gather = bf16[4,1,512]{2,1,0:T(2,128)(2,1)S(1)} all-gather(bf16[1,1,512]{2,1,0:T(2,128)(2,1)S(1)} %reshape.296), channel_id=1, replica_groups=mesh['row'=4,'col'=8] {'row'}, dimensions={0}, use_global_device_ids=true | all-gather | bytes 5120 | tf_op jit(solution)/shard_map/all_gather | solution.py:180
  26.1 23.9 %all-gather.14.cloned.1.call-done = bf16[1024,2048]{1,0:T(8,128)(2,1)} async-done(((bf16[1024,256]{1,0:T(8,128)(2,1)}), bf16[1024,2048]{1,0:T(8,128)(2,1)}) %all-gather.14.cloned.1.call-update) | async-done | bytes 4194320 | tf_op jit(solution)/shard_map/all_gather | solution.py:198
  56.6 23.0 %all-gather.18.cloned.1.call-done = bf16[2048,256]{1,0:T(8,128)(2,1)} async-done(((bf16[512,256]{1,0:T(8,128)(2,1)}), bf16[2048,256]{1,0:T(8,128)(2,1)}) %all-gather.18.cloned.1.call-update) | async-done | bytes 1048592 | tf_op jit(solution)/shard_map/all_gather | solution.py:174
  83.4 25.3 %all-gather.16.cloned.1.call-done = bf16[2048,256]{1,0:T(8,128)(2,1)} async-done(((bf16[512,256]{1,0:T(8,128)(2,1)}), bf16[2048,256]{1,0:T(8,128)(2,1)}) %all-gather.16.cloned.1.call-update) | async-done | bytes 1048592 | tf_op jit(solution)/shard_map/all_gather | solution.py:173
  112.8 24.7 %all-gather.20.cloned.1.call-done = bf16[2048,256]{1,0:T(8,128)(2,1)} async-done(((bf16[512,256]{1,0:T(8,128)(2,1)}), bf16[2048,256]{1,0:T(8,128)(2,1)}) %all-gather.20.cloned.1.call-update) | async-done | bytes 1048592 | tf_op jit(solution)/shard_map/all_gather | solution.py:175
  141.3 18.4 %while.31 = (s32[]{:T(128)}, bf16[2,512,4,64]{1,3,2,0:T(8,128)(2,1)S(1)}, f32[2,4,512]{2,1,0:T(4,128)S(1)}, s32[2]{0:T(128)S(1)}, s32[1024]{0:T(1024)S(1)}, /*in...) while((s32[]{:T(128)}, ...), condition=%wide.region_4.5_spmd, body=%wide.region_1.4_spmd.sunk | while | flops 563740160 | bytes 28924288 | solution.py:101
  172.3 70.9 %reduce-scatter.12.cloned.1.call-done = f32[1024,256]{1,0:T(8,128)} async-done(((f32[1024,2048]{1,0:T(8,128)}), f32[1024,256]{1,0:T(8,128)}) %reduce-scatter.12.cloned.1.call-update) | async-done | bytes 1048592 | tf_op jit(solution)/shard_map/reduce_scatter | solution.py:219
  248.4 12.1 %all-gather.1 = bf16[4,1,512]{2,1,0:T(2,128)(2,1)S(1)} all-gather(bf16[1,1,512]{2,1,0:T(2,128)(2,1)S(1)} %reshape.298), channel_id=1, replica_groups=mesh['row'=4,'col'=8] {'row'}, dimensions={0}, use_global_device_ids=true | all-gather | bytes 5120 | tf_op jit(solution)/shard_map/all_gather | solution.py:181
  260.5 41.1 %all-gather.24.cloned.1.call-done = f32[1024,2048]{1,0:T(8,128)} async-done(((f32[1024,256]{1,0:T(8,128)}), f32[1024,2048]{1,0:T(8,128)}) %all-gather.24.cloned.1.call-update) | async-done | bytes 8388624 | tf_op jit(solution)/shard_map/all_gather | solution.py:221
  313.4 70.6 %all-gather.28.cloned.1.call-done = bf16[2048,1024]{1,0:T(8,128)(2,1)} async-done(((bf16[512,1024]{1,0:T(8,128)(2,1)}), bf16[2048,1024]{1,0:T(8,128)(2,1)}) %all-gather.28.cloned.1.call-update) | async-done | bytes 4194320 | tf_op jit(solution)/shard_map/all_gather | solution.py:178
  384.0 9.9 fusion.43
  393.9 71.1 %all-gather.26.cloned.1.call-done = bf16[2048,1024]{1,0:T(8,128)(2,1)} async-done(((bf16[512,1024]{1,0:T(8,128)(2,1)}), bf16[2048,1024]{1,0:T(8,128)(2,1)}) %all-gather.26.cloned.1.call-update) | async-done | bytes 4194320 | tf_op jit(solution)/shard_map/all_gather | solution.py:177
  465.0 10.0 fusion.42
  475.0 70.8 %all-gather.30.cloned.1.call-done = bf16[2048,1024]{1,0:T(8,128)(2,1)} async-done(((bf16[512,1024]{1,0:T(8,128)(2,1)}), bf16[2048,1024]{1,0:T(8,128)(2,1)}) %all-gather.30.cloned.1.call-update) | async-done | bytes 4194320 | tf_op jit(solution)/shard_map/all_gather | solution.py:179
  545.8 38.0 %all-gather.32.cloned.1.call-done = bf16[1024,2048]{1,0:T(8,128)(2,1)} async-done(((bf16[1024,256]{1,0:T(8,128)(2,1)}), bf16[1024,2048]{1,0:T(8,128)(2,1)}) %all-gather.32.cloned.1.call-update) | async-done | bytes 4194320 | tf_op jit(solution)/shard_map/all_gather | solution.py:235
  583.9 14.0 %multiply_convert_fusion.3 = (bf16[1024,1024]{1,0:T(8,128)(2,1)}, bf16[1024,1024]{1,0:T(8,128)(2,1)S(1)}, bf16[1024,1024]{1,0:T(8,128)(2,1)}) fusion(f32[1024,1024]{1,0:T(8,128)} %fusion.42, f32[1024,1024]{1,0:T(8,128)} %fusion.43, bf16[1024,2048]{1,0:T(8,128)(2,1)} %all-gather.32.cloned.1.call-done, bf16[2048,1024]{1,0:T(8,128)(2,1)} %all-gather.30.cloned.1.call-done), kind=kOutput, calls=%fused_computation.59 | convolution fusion | flops 4310695936 | bytes 23068672 | tf_op jit(solution)/shard_map/dot_general | solution.py:236
  604.9 11.7 multiply_reduce_fusion.1
  616.8 13.1 %psum.28 = f32[1024]{0:T(1024)S(1)} all-reduce(f32[1024]{0:T(1024)S(1)} %get-tuple-element.329), channel_id=1, replica_groups=mesh['row'=4,'col'=8] {'col'}, use_global_device_ids=true, to_apply=%region_10.11 | all-reduce | flops 1024 | bytes 8192 | tf_op jit(solution)/shard_map/psum | solution.py:247
  629.9 38.2 %reduce-scatter.16.cloned.1.call-done = bf16[1024,256]{1,0:T(8,128)(2,1)} async-done(((bf16[1024,2048]{1,0:T(8,128)(2,1)}), bf16[1024,256]{1,0:T(8,128)(2,1)}) %reduce-scatter.16.cloned.1.call-update) | async-done | bytes 524304 | tf_op jit(solution)/shard_map/reduce_scatter | solution.py:248
  690.0 9.7 convolution_convert_fusion
  718.9 54.1 %while.32 = (s32[]{:T(128)}, f32[1024,4,64]{0,2,1:T(8,128)S(1)}, f32[1024,4,64]{0,2,1:T(8,128)}, f32[2,512,4,64]{1,0,3,2:T(2,128)}, s32[2]{0:T(128)S(1)}, /*inde...) while((s32[]{:T(128)}, f32[1024,4,64]{0,2,1:T(8,128)S(1)}, ...), condition=%wide.region_13.14_spmd.clone, body=%wide.region_11.13_spmd.clone.sunk | while | flops 1376648704 | bytes 82917864 | solution.py:146
  735.5 10.4 dynamic_update_slice.29
  762.6 10.4 dynamic_update_slice.29
  805.8 36.1 %reduce-scatter.32.cloned.1.call-done = bf16[512,1024]{0,1:T(8,128)(2,1)} async-done(((bf16[2048,1024]{0,1:T(8,128)(2,1)}), bf16[512,1024]{0,1:T(8,128)(2,1)}) %reduce-scatter.32.cloned.1.call-update) | async-done | bytes 1048592 | tf_op jit(solution)/shard_map/reduce_scatter | solution.py:318
  844.5 76.9 %reduce-scatter.30.cloned.1.call-done = bf16[512,1024]{1,0:T(8,128)(2,1)} async-done(((bf16[2048,1024]{1,0:T(8,128)(2,1)}), bf16[512,1024]{1,0:T(8,128)(2,1)}) %reduce-scatter.30.cloned.1.call-update) | async-done | bytes 1048592 | tf_op jit(solution)/shard_map/reduce_scatter | solution.py:315
  924.1 76.8 %reduce-scatter.28.cloned.1.call-done = bf16[512,1024]{1,0:T(8,128)(2,1)} async-done(((bf16[2048,1024]{1,0:T(8,128)(2,1)}), bf16[512,1024]{1,0:T(8,128)(2,1)}) %reduce-scatter.28.cloned.1.call-update) | async-done | bytes 1048592 | tf_op jit(solution)/shard_map/reduce_scatter | solution.py:312
  1003.7 25.2 %all-reduce.2 = (f32[1024]{0:T(1024)S(1)}, bf16[2048]{0:T(1024)(128)(2,1)S(1)}, bf16[2048]{0:T(1024)(128)(2,1)S(1)}) all-reduce(f32[1024]{0:T(1024)S(1)} %get-tuple-element.331, f32[2048]{0:T(1024)S(1)} %get-tuple-element.330, f32[2048]{0:T(1024)S(1)} %copy-done.28), channel_id=1, replica_groups=mesh['row'=4,'col'=8] {'col'}, use_global_device_ids=true, to_apply=%region_16.17 | all-reduce | flops 5120 | bytes 32768 | tf_op jit(solution)/shard_map/psum | solution.py:289
  1028.9 11.4 all-reduce.3
  1043.4 15.5 %reduce-scatter.24.cloned.1.call-done = bf16[512,256]{1,0:T(8,128)(2,1)} async-done(((bf16[2048,256]{1,0:T(8,128)(2,1)}), bf16[512,256]{1,0:T(8,128)(2,1)}) %reduce-scatter.24.cloned.1.call-update) | async-done | bytes 262160 | tf_op jit(solution)/shard_map/reduce_scatter | solution.py:306
  1060.7 26.2 %reduce-scatter.20.cloned.1.call-done = bf16[512,256]{1,0:T(8,128)(2,1)} async-done(((bf16[2048,256]{1,0:T(8,128)(2,1)}), bf16[512,256]{1,0:T(8,128)(2,1)}) %reduce-scatter.20.cloned.1.call-update) | async-done | bytes 262160 | tf_op jit(solution)/shard_map/reduce_scatter | solution.py:300
  1088.7 26.5 %reduce-scatter.22.cloned.1.call-done = bf16[512,256]{1,0:T(8,128)(2,1)} async-done(((bf16[2048,256]{1,0:T(8,128)(2,1)}), bf16[512,256]{1,0:T(8,128)(2,1)}) %reduce-scatter.22.cloned.1.call-update) | async-done | bytes 262160 | tf_op jit(solution)/shard_map/reduce_scatter | solution.py:303
  1116.9 51.6 %reduce-scatter.18.cloned.1.call-done = bf16[1024,256]{1,0:T(8,128)(2,1)} async-done(((bf16[1024,2048]{1,0:T(8,128)(2,1)}), bf16[1024,256]{1,0:T(8,128)(2,1)}) %reduce-scatter.18.cloned.1.call-update) | async-done | bytes 524304 | tf_op jit(solution)/shard_map/reduce_scatter | solution.py:290
  (227 shorter events, 200.6 us)
Async XLA Ops:
  7.2 42.9 %all-gather.14.cloned.1.call-start = ((), (), s32[]{:S(2)}) async-start(), calls=%async_computation.11 | async-start | bytes 4718592 | tf_op jit(solution)/shard_map/all_gather | solution.py:198
  7.9 71.7 %all-gather.18.cloned.1.call-start = ((), (), s32[]{:S(2)}) async-start(), calls=%async_computation.13 | async-start | bytes 1310720 | tf_op jit(solution)/shard_map/all_gather | solution.py:174
  8.7 100.0 %all-gather.16.cloned.1.call-start = ((), (), s32[]{:S(2)}) async-start(), calls=%async_computation.12 | async-start | bytes 1310720 | tf_op jit(solution)/shard_map/all_gather | solution.py:173
  9.4 128.1 %all-gather.20.cloned.1.call-start = ((), (), s32[]{:S(2)}) async-start(), calls=%async_computation.14 | async-start | bytes 1310720 | tf_op jit(solution)/shard_map/all_gather | solution.py:175
  10.0 156.4 %all-gather.22.cloned.1.call-start = ((), (), s32[]{:S(2)}) async-start(), calls=%async_computation.15 | async-start | bytes 1310720 | tf_op jit(solution)/shard_map/all_gather | solution.py:176
  10.6 232.6 %reduce-scatter.12.cloned.1.call-start = ((), (), s32[]{:S(2)}) async-start(), calls=%async_computation.16 | async-start | bytes 9437184 | tf_op jit(solution)/shard_map/reduce_scatter | solution.py:219
  26.1 86.3 %copy-start.8 = (f32[1024,32]{0,1:T(8,128)}, f32[1024,32]{0,1:T(8,128)S(1)}, u32[]{:S(2)}) copy-start(f32[1024,32]{0,1:T(8,128)S(1)} %get-tuple-element.399) | copy-start | bytes 393220
  26.1 86.3 %copy-start.10 = (f32[1024,32]{0,1:T(8,128)}, f32[1024,32]{0,1:T(8,128)S(1)}, u32[]{:S(2)}) copy-start(f32[1024,32]{0,1:T(8,128)S(1)} %get-tuple-element.400) | copy-start | bytes 393220
  172.2 76.1 %copy-start.29 = (bf16[512]{0:T(512)(128)(2,1)S(1)}, bf16[512]{0:T(512)(128)(2,1)}, u32[]{:S(2)}) copy-start(bf16[512]{0:T(512)(128)(2,1)} %param.26) | copy-start | bytes 3076
  172.2 129.3 %all-gather.24.cloned.1.call-start = ((), (), s32[]{:S(2)}) async-start(), calls=%async_computation.17 | async-start | bytes 9437184 | tf_op jit(solution)/shard_map/all_gather | solution.py:221
  245.5 138.5 %all-gather.28.cloned.1.call-start = ((), (), s32[]{:S(2)}) async-start(), calls=%async_computation.19 | async-start | bytes 5242880 | tf_op jit(solution)/shard_map/all_gather | solution.py:178
  246.2 218.8 %all-gather.26.cloned.1.call-start = ((), (), s32[]{:S(2)}) async-start(), calls=%async_computation.18 | async-start | bytes 5242880 | tf_op jit(solution)/shard_map/all_gather | solution.py:177
  247.0 298.8 %all-gather.30.cloned.1.call-start = ((), (), s32[]{:S(2)}) async-start(), calls=%async_computation.20 | async-start | bytes 5242880 | tf_op jit(solution)/shard_map/all_gather | solution.py:179
  247.6 336.3 %all-gather.32.cloned.1.call-start = ((), (), s32[]{:S(2)}) async-start(), calls=%async_computation.22 | async-start | bytes 4718592 | tf_op jit(solution)/shard_map/all_gather | solution.py:235
  248.3 419.8 %reduce-scatter.16.cloned.1.call-start = ((), (), s32[]{:S(2)}) async-start(), calls=%async_computation.23 | async-start | bytes 4718592 | tf_op jit(solution)/shard_map/reduce_scatter | solution.py:248
  305.7 362.4 %copy-start.22 = (f32[1024]{0:T(1024)}, f32[1024]{0:T(1024)S(1)}, u32[]{:S(2)}) copy-start(f32[1024]{0:T(1024)S(1)} %add_rsqrt_fusion) | copy-start | bytes 12292
  616.7 92.9 %all-gather.34.cloned.1.call-start = ((), (), s32[]{:S(2)}) async-start(), calls=%async_computation.24 | async-start | bytes 4718592 | tf_op jit(solution)/shard_map/all_gather | solution.py:255
  670.7 133.1 %reduce-scatter.14.cloned.1.call-start = ((), (), s32[]{:S(2)}) async-start(), calls=%async_computation.21 | async-start | bytes 4718592 | tf_op jit(solution)/shard_map/reduce_scatter | solution.py:231
  680.1 161.7 %reduce-scatter.32.cloned.1.call-start = ((), (), s32[]{:S(2)}) async-start(), calls=%async_computation.32 | async-start | bytes 5242880 | tf_op jit(solution)/shard_map/reduce_scatter | solution.py:318
  690.0 231.3 %reduce-scatter.30.cloned.1.call-start = ((), (), s32[]{:S(2)}) async-start(), calls=%async_computation.31 | async-start | bytes 5242880 | tf_op jit(solution)/shard_map/reduce_scatter | solution.py:315
  699.8 301.1 %reduce-scatter.28.cloned.1.call-start = ((), (), s32[]{:S(2)}) async-start(), calls=%async_computation.30 | async-start | bytes 5242880 | tf_op jit(solution)/shard_map/reduce_scatter | solution.py:312
  709.5 332.2 %reduce-scatter.26.cloned.1.call-start = ((), (), s32[]{:S(2)}) async-start(), calls=%async_computation.29 | async-start | bytes 1310720 | tf_op jit(solution)/shard_map/reduce_scatter | solution.py:309
  714.1 344.8 %reduce-scatter.24.cloned.1.call-start = ((), (), s32[]{:S(2)}) async-start(), calls=%async_computation.28 | async-start | bytes 1310720 | tf_op jit(solution)/shard_map/reduce_scatter | solution.py:306
  778.9 308.0 %reduce-scatter.20.cloned.1.call-start = ((), (), s32[]{:S(2)}) async-start(), calls=%async_computation.26 | async-start | bytes 1310720 | tf_op jit(solution)/shard_map/reduce_scatter | solution.py:300
  785.9 329.2 %reduce-scatter.22.cloned.1.call-start = ((), (), s32[]{:S(2)}) async-start(), calls=%async_computation.27 | async-start | bytes 1310720 | tf_op jit(solution)/shard_map/reduce_scatter | solution.py:303
  790.6 377.9 %reduce-scatter.18.cloned.1.call-start = ((), (), s32[]{:S(2)}) async-start(), calls=%async_computation.25 | async-start | bytes 4718592 | tf_op jit(solution)/shard_map/reduce_scatter | solution.py:290
  805.8 197.9 %copy-start.28 = (f32[2048]{0:T(1024)S(1)}, f32[2048]{0:T(1024)}, u32[]{:S(2)}) copy-start(f32[2048]{0:T(1024)} %get-tuple-element.328) | copy-start | bytes 24580
  844.4 324.0 %copy-start.4 = (bf16[1024,256]{1,0:T(8,128)(2,1)S(1)}, bf16[1024,256]{1,0:T(8,128)(2,1)}, u32[]{:S(2)}) copy-start(bf16[1024,256]{1,0:T(8,128)(2,1)} %param.29) | copy-start | bytes 1572868
  844.4 324.0 %copy-start.7 = (bf16[1024,256]{1,0:T(8,128)(2,1)S(1)}, bf16[1024,256]{1,0:T(8,128)(2,1)}, u32[]{:S(2)}) copy-start(bf16[1024,256]{1,0:T(8,128)(2,1)} %reduce-scatter.16.cloned.1.call-done) | copy-start | bytes 1572868
  844.4 324.0 %copy-start.23 = (f32[1024]{0:T(1024)S(1)}, f32[1024]{0:T(1024)}, u32[]{:S(2)}) copy-start(f32[1024]{0:T(1024)} %copy-done.22) | copy-start | bytes 12292
  844.5 324.0 %copy-start.25 = (f32[1024]{0:T(1024)S(1)}, f32[1024]{0:T(1024)}, u32[]{:S(2)}) copy-start(f32[1024]{0:T(1024)} %copy-done.24) | copy-start | bytes 12292
  844.5 324.0 %copy-start.27 = (f32[256]{0:T(256)S(1)}, f32[256]{0:T(256)}, u32[]{:S(2)}) copy-start(f32[256]{0:T(256)} %copy-done.26) | copy-start | bytes 3076
  (26 other events, 376.7 us)
Sparse Core Ops, SparseCore 0:
  9.9 40.1 all-gather.13
  51.6 27.9 all-gather.17
  81.2 27.4 all-gather.15
  110.0 27.4 all-gather.19
  138.9 27.4 all-gather.21
  172.3 70.7 reduce-scatter.11
  245.6 55.9 all-gather.23
  303.2 80.7 all-gather.27
  385.7 79.2 all-gather.25
  466.5 79.2 all-gather.29
  547.9 35.9 all-gather.31
  616.8 51.3 reduce-scatter.15
  670.8 37.4 all-gather.33
  711.5 51.3 reduce-scatter.13
  765.1 76.7 reduce-scatter.31
  844.0 77.2 reduce-scatter.29
  923.6 77.2 reduce-scatter.27
  1003.0 27.6 reduce-scatter.25
  1033.1 25.7 reduce-scatter.23
  1061.1 25.7 reduce-scatter.19
  1089.3 25.7 reduce-scatter.21
  1118.5 49.9 reduce-scatter.17
where the time goes:
time: 1190 us; the launch traced here: 1180 us
  waiting for transfers between devices  819 us (69%)
  matrix products  173 us (15%)
  blocking collectives  75.4 us (6%)
  other arithmetic  54.9 us (5%)
  local copies, waits for them, and re-layouts  35.6 us (3%)
  between operations  15.7 us (1%)
    reduce_scatter x1, waiting for transfers between devices, local(): lax.psum_scatter(up_weight_grad.astype(jnp.bfloat16), 'row', scatter_dime...  76.9 us
    reduce_scatter x1, waiting for transfers between devices, local(): lax.psum_scatter(gate_weight_grad.astype(jnp.bfloat16), 'row', scatter_di...  76.8 us
    all_gather x1, waiting for transfers between devices, local(): lax.all_gather(gate_weight, 'row', axis=0, tiled=True)  71.1 us
    reduce_scatter x1, waiting for transfers between devices, local(): lax.psum_scatter(attention_part, 'col', scatter_dimension=1, tiled=True)  70.9 us
    all_gather x1, waiting for transfers between devices, local(): lax.all_gather(down_weight, 'row', axis=0, tiled=True)  70.8 us
    all_gather x1, waiting for transfers between devices, local(): lax.all_gather(up_weight, 'row', axis=0, tiled=True)  70.6 us
    reduce_scatter x1, waiting for transfers between devices, local(): lax.psum_scatter(normed_one_grad.astype(jnp.bfloat16), 'col', scatter_dim...  51.6 us
    dot_general x7, matrix products, contract_last(): lax.dot_general(left, right, (((1,), (1,)), ((), ())), preferred_element_...  45.1 us
  transfers between devices with their start and end apart: 22, of which 19 were waited for; matrix products, arithmetic and copies ran while one was open for 18% of the time, Pallas kernels for 0%

commit v1 on v0

--- a/solution.py
+++ b/solution.py
@@ -218,7 +218,12 @@
     attention_part = contract_last(mixed, out_full)
     attention_block = lax.psum_scatter(attention_part, "col", scatter_dimension=1, tiled=True)
     middle_block = input_block + attention_block
-    middle_rows = lax.all_gather(middle_block, "col", axis=1, tiled=True)
+    ring = [middle_block]
+    for hop in range(7):
+        ring.append(lax.ppermute(ring[-1], "col", [(dev, (dev + 1) % 8) for dev in range(8)]))
+    middle_rows = jnp.roll(
+        jnp.concatenate(ring[::-1], axis=1), (lax.axis_index("col") + 1) * ring[0].shape[1], axis=1
+    )
     scale_two = lax.rsqrt(jnp.mean(middle_rows * middle_rows, axis=1, keepdims=True) + eps)
     unit_two = middle_rows * scale_two
     normed_two = (unit_two * gain_two).astype(jnp.bfloat16)

time: 1190 us -> 1140 us (0.958)
  waiting for transfers between devices: 819 us -> 730 us
  matrix products: 173 us -> 193 us
  local copies, waits for them, and re-layouts: 35.6 us -> 54.9 us
    ppermute x0 -> x7, waiting for transfers between devices: none -> 83.5 us  [local(): lax.ppermute(ring[-1], 'col', [(dev, (dev + 1) % 8) for dev in range(8)])]
    all_gather x1, waiting for transfers between devices: 70.8 us -> 0.02 us  [local(): lax.all_gather(down_weight, 'row', axis=0, tiled=True)]
    reduce_scatter x1, waiting for transfers between devices: 76.8 us -> 14.1 us  [local(): lax.psum_scatter(gate_weight_grad.astype(jnp.bfloat16), 'row', scatter_di...]
    all_gather x1 -> x0, waiting for transfers between devices: 41.1 us -> none  [local(): middle_rows = lax.all_gather(middle_block, 'col', axis=1, tiled=True)]
    reduce_scatter x1, waiting for transfers between devices: 36.1 us -> 76.8 us  [local(): lax.psum_scatter(down_weight_grad.astype(jnp.bfloat16), 'row', scatter_di...]
    reduce_scatter x1, waiting for transfers between devices: 0.01 us -> 26.3 us  [local(): lax.psum_scatter(out_weight_grad.astype(jnp.bfloat16), 'row', scatter_dim...]
    reduce_scatter x1, waiting for transfers between devices: 26.2 us -> 0.01 us  [local(): lax.psum_scatter(query_weight_grad.astype(jnp.bfloat16), 'row', scatter_d...]
    all_gather x1, waiting for transfers between devices: 70.6 us -> 45.8 us  [local(): lax.all_gather(up_weight, 'row', axis=0, tiled=True)]
  transfers between devices with their start and end apart: 22 -> 28, of which waited for: 19 -> 23; matrix products, arithmetic and copies ran while one was open for 18% -> 22% of each run, Pallas kernels for 0% -> 0%
where the time goes in v1:
time: 1140 us; the launch traced here: 1130 us
  waiting for transfers between devices  730 us (64%)
  matrix products  193 us (17%)
  blocking collectives  75.7 us (7%)
  other arithmetic  56.1 us (5%)
  local copies, waits for them, and re-layouts  54.9 us (5%)
  between operations  15.9 us (1%)
    ppermute x7, waiting for transfers between devices, local(): lax.ppermute(ring[-1], 'col', [(dev, (dev + 1) % 8) for dev in range(8)])  83.5 us
    reduce_scatter x1, waiting for transfers between devices, local(): lax.psum_scatter(down_weight_grad.astype(jnp.bfloat16), 'row', scatter_di...  76.8 us
    reduce_scatter x1, waiting for transfers between devices, local(): lax.psum_scatter(up_weight_grad.astype(jnp.bfloat16), 'row', scatter_dime...  76.6 us
    all_gather x1, waiting for transfers between devices, local(): lax.all_gather(gate_weight, 'row', axis=0, tiled=True)  70.9 us
    reduce_scatter x1, waiting for transfers between devices, local(): lax.psum_scatter(attention_part, 'col', scatter_dimension=1, tiled=True)  68.6 us
    reduce_scatter x1, waiting for transfers between devices, local(): lax.psum_scatter(normed_one_grad.astype(jnp.bfloat16), 'col', scatter_dim...  51.6 us
    dot_general x7, matrix products, contract_last(): lax.dot_general(left, right, (((1,), (1,)), ((), ())), preferred_element_...  47.8 us
    all_gather x1, waiting for transfers between devices, local(): lax.all_gather(up_weight, 'row', axis=0, tiled=True)  45.8 us
  transfers between devices with their start and end apart: 28, of which 23 were waited for; matrix products, arithmetic and copies ran while one was open for 22% of the time, Pallas kernels for 0%

profile of v1, /device:TPU:0, one launch (start us, length us, event | category | flops | bytes accessed | tf_op | source)
XLA Modules:
  0.0 1130.2 jit_solution(5721128677385392574)
XLA Ops:
  11.3 13.5 %all-gather = bf16[4,1,512]{2,1,0:T(2,128)(2,1)S(1)} all-gather(bf16[1,1,512]{2,1,0:T(2,128)(2,1)S(1)} %reshape.296), channel_id=1, replica_groups=mesh['row'=4,'col'=8] {'row'}, dimensions={0}, use_global_device_ids=true | all-gather | bytes 5120 | tf_op jit(solution)/shard_map/all_gather | solution.py:180
  26.1 23.9 %all-gather.13.cloned.1.call-done = bf16[1024,2048]{1,0:T(8,128)(2,1)} async-done(((bf16[1024,256]{1,0:T(8,128)(2,1)}), bf16[1024,2048]{1,0:T(8,128)(2,1)}) %all-gather.13.cloned.1.call-update) | async-done | bytes 4194320 | tf_op jit(solution)/shard_map/all_gather | solution.py:198
  56.5 23.1 %all-gather.17.cloned.1.call-done = bf16[2048,256]{1,0:T(8,128)(2,1)} async-done(((bf16[512,256]{1,0:T(8,128)(2,1)}), bf16[2048,256]{1,0:T(8,128)(2,1)}) %all-gather.17.cloned.1.call-update) | async-done | bytes 1048592 | tf_op jit(solution)/shard_map/all_gather | solution.py:174
  83.4 25.3 %all-gather.15.cloned.1.call-done = bf16[2048,256]{1,0:T(8,128)(2,1)} async-done(((bf16[512,256]{1,0:T(8,128)(2,1)}), bf16[2048,256]{1,0:T(8,128)(2,1)}) %all-gather.15.cloned.1.call-update) | async-done | bytes 1048592 | tf_op jit(solution)/shard_map/all_gather | solution.py:173
  112.8 24.7 %all-gather.19.cloned.1.call-done = bf16[2048,256]{1,0:T(8,128)(2,1)} async-done(((bf16[512,256]{1,0:T(8,128)(2,1)}), bf16[2048,256]{1,0:T(8,128)(2,1)}) %all-gather.19.cloned.1.call-update) | async-done | bytes 1048592 | tf_op jit(solution)/shard_map/all_gather | solution.py:175
  141.3 18.1 %while.31 = (s32[]{:T(128)}, bf16[2,512,4,64]{1,3,2,0:T(8,128)(2,1)S(1)}, f32[2,4,512]{2,1,0:T(4,128)S(1)}, s32[2]{0:T(128)S(1)}, s32[1024]{0:T(1024)S(1)}, /*in...) while((s32[]{:T(128)}, ...), condition=%wide.region_4.5_spmd, body=%wide.region_1.4_spmd.sunk | while | flops 563740160 | bytes 28924288 | solution.py:101
  174.5 68.6 %reduce-scatter.12.cloned.1.call-done = f32[1024,256]{1,0:T(8,128)} async-done(((f32[1024,2048]{1,0:T(8,128)}), f32[1024,256]{1,0:T(8,128)}) %reduce-scatter.12.cloned.1.call-update) | async-done | bytes 1048592 | tf_op jit(solution)/shard_map/reduce_scatter | solution.py:219
  244.6 15.1 %collective-permute-done = f32[1024,256]{1,0:T(8,128)S(1)} collective-permute-done((f32[1024,256]{1,0:T(8,128)S(1)}, f32[1024,256]{1,0:T(8,128)S(1)}, u32[]{:S(2)}, u32[]{:S(2)}) %collective-permute-start) | collective-permute-done | bytes 1048608 | tf_op jit(solution)/shard_map/ppermute | solution.py:223
  260.7 15.1 %collective-permute-done.1 = f32[1024,256]{1,0:T(8,128)S(1)} collective-permute-done((f32[1024,256]{1,0:T(8,128)S(1)}, f32[1024,256]{1,0:T(8,128)S(1)}, u32[]{:S(2)}, u32[]{:S(2)}) %collective-permute-start.1) | collective-permute-done | bytes 1048608 | tf_op jit(solution)/shard_map/ppermute | solution.py:223
  276.8 15.1 %collective-permute-done.2 = f32[1024,256]{1,0:T(8,128)S(1)} collective-permute-done((f32[1024,256]{1,0:T(8,128)S(1)}, f32[1024,256]{1,0:T(8,128)S(1)}, u32[]{:S(2)}, u32[]{:S(2)}) %collective-permute-start.2) | collective-permute-done | bytes 1048608 | tf_op jit(solution)/shard_map/ppermute | solution.py:223
  292.9 15.1 %collective-permute-done.3 = f32[1024,256]{1,0:T(8,128)S(1)} collective-permute-done((f32[1024,256]{1,0:T(8,128)S(1)}, f32[1024,256]{1,0:T(8,128)S(1)}, u32[]{:S(2)}, u32[]{:S(2)}) %collective-permute-start.3) | collective-permute-done | bytes 1048608 | tf_op jit(solution)/shard_map/ppermute | solution.py:223
  309.0 15.2 %collective-permute-done.4 = f32[1024,256]{1,0:T(8,128)} collective-permute-done((f32[1024,256]{1,0:T(8,128)S(1)}, f32[1024,256]{1,0:T(8,128)}, u32[]{:S(2)}, u32[]{:S(2)}) %collective-permute-start.4) | collective-permute-done | bytes 1048608 | tf_op jit(solution)/shard_map/ppermute | solution.py:223
  324.3 11.9 %all-gather.1 = bf16[4,1,512]{2,1,0:T(2,128)(2,1)S(1)} all-gather(bf16[1,1,512]{2,1,0:T(2,128)(2,1)S(1)} %reshape.298), channel_id=1, replica_groups=mesh['row'=4,'col'=8] {'row'}, dimensions={0}, use_global_device_ids=true | all-gather | bytes 5120 | tf_op jit(solution)/shard_map/all_gather | solution.py:181
  344.2 28.6 %all-gather.29.cloned.1.call-done = bf16[1024,2048]{1,0:T(8,128)(2,1)} async-done(((bf16[1024,256]{1,0:T(8,128)(2,1)}), bf16[1024,2048]{1,0:T(8,128)(2,1)}) %all-gather.29.cloned.1.call-update) | async-done | bytes 4194320 | tf_op jit(solution)/shard_map/all_gather | solution.py:240
  408.6 45.8 %all-gather.25.cloned.1.call-done = bf16[2048,1024]{1,0:T(8,128)(2,1)} async-done(((bf16[512,1024]{1,0:T(8,128)(2,1)}), bf16[2048,1024]{1,0:T(8,128)(2,1)}) %all-gather.25.cloned.1.call-update) | async-done | bytes 4194320 | tf_op jit(solution)/shard_map/all_gather | solution.py:178
  464.3 70.9 %all-gather.23.cloned.1.call-done = bf16[2048,1024]{1,0:T(8,128)(2,1)} async-done(((bf16[512,1024]{1,0:T(8,128)(2,1)}), bf16[2048,1024]{1,0:T(8,128)(2,1)}) %all-gather.23.cloned.1.call-update) | async-done | bytes 4194320 | tf_op jit(solution)/shard_map/all_gather | solution.py:177
  535.2 14.6 %multiply_convert_fusion.3 = (bf16[1024,1024]{1,0:T(8,128)(2,1)}, bf16[1024,1024]{1,0:T(8,128)(2,1)S(1)}, bf16[1024,1024]{1,0:T(8,128)(2,1)}) fusion(f32[1024,1024]{1,0:T(8,128)} %fusion.43, f32[1024,1024]{1,0:T(8,128)} %fusion.42, bf16[1024,2048]{1,0:T(8,128)(2,1)} %get-tuple-element.375, bf16[2048,1024]{1,0:T(8,128)(2,1)} %all-gather.23.cloned.1.call-done), kind=kOutput, calls=%fused_computation.60 | convolution fusion | flops 4310695936 | bytes 23068672 | tf_op jit(solution)/shard_map/dot_general | solution.py:230
  556.6 13.3 %multiply_reduce_fusion.1 = (f32[2048]{0:T(1024)}, f32[1024]{0:T(1024)S(1)}, bf16[1024,2048]{1,0:T(8,128)(2,1)}) fusion(f32[1024,2048]{1,0:T(8,128)S(1)} %copy-done.5, f32[2048]{0:T(1024)S(1)} %bitcast.141, f32[1024,2048]{1,0:T(8,128)} %fusion.44, bf16[1024,1024]{1,0:T(8,128)(2,1)} %get-tuple-element.383, bf16[2048,1024]{1,0:T(8,128)(2,1)} %all-gather.25.cloned.1.call-done), kind=kOutput, calls=%fused_computation.50 | convolution fusion | flops 4309644288 | bytes 27283456 | tf_op jit(solution)/shard_map/dot_general | solution.py:53
  570.1 13.6 %psum.28 = f32[1024]{0:T(1024)S(1)} all-reduce(f32[1024]{0:T(1024)S(1)} %get-tuple-element.329), channel_id=1, replica_groups=mesh['row'=4,'col'=8] {'col'}, use_global_device_ids=true, to_apply=%region_10.11 | all-reduce | flops 1024 | bytes 8192 | tf_op jit(solution)/shard_map/psum | solution.py:252
  583.7 36.2 %reduce-scatter.16.cloned.1.call-done = bf16[1024,256]{1,0:T(8,128)(2,1)} async-done(((bf16[1024,2048]{1,0:T(8,128)(2,1)}), bf16[1024,256]{1,0:T(8,128)(2,1)}) %reduce-scatter.16.cloned.1.call-update) | async-done | bytes 524304 | tf_op jit(solution)/shard_map/reduce_scatter | solution.py:253
  665.5 75.5 %while.32 = (s32[]{:T(128)}, f32[1024,4,64]{0,2,1:T(8,128)S(1)}, f32[1024,4,64]{0,2,1:T(8,128)}, f32[2,512,4,64]{1,0,3,2:T(2,128)}, s32[2]{0:T(128)S(1)}, /*inde...) while((s32[]{:T(128)}, f32[1024,4,64]{0,2,1:T(8,128)S(1)}, ...), condition=%wide.region_13.14_spmd.clone, body=%wide.region_11.13_spmd.clone.sunk | while | flops 1376648704 | bytes 126958168 | solution.py:146
  693.5 10.4 dynamic_update_slice.29
  730.6 10.4 dynamic_update_slice.29
  779.7 14.1 %reduce-scatter.28.cloned.1.call-done = bf16[512,1024]{1,0:T(8,128)(2,1)} async-done(((bf16[2048,1024]{1,0:T(8,128)(2,1)}), bf16[512,1024]{1,0:T(8,128)(2,1)}) %reduce-scatter.28.cloned.1.call-update) | async-done | bytes 1048592 | tf_op jit(solution)/shard_map/reduce_scatter | solution.py:317
  796.6 76.6 %reduce-scatter.30.cloned.1.call-done = bf16[512,1024]{1,0:T(8,128)(2,1)} async-done(((bf16[2048,1024]{1,0:T(8,128)(2,1)}), bf16[512,1024]{1,0:T(8,128)(2,1)}) %reduce-scatter.30.cloned.1.call-update) | async-done | bytes 1048592 | tf_op jit(solution)/shard_map/reduce_scatter | solution.py:320
  876.0 76.8 %reduce-scatter.32.cloned.1.call-done = bf16[512,1024]{0,1:T(8,128)(2,1)} async-done(((bf16[2048,1024]{0,1:T(8,128)(2,1)}), bf16[512,1024]{0,1:T(8,128)(2,1)}) %reduce-scatter.32.cloned.1.call-update) | async-done | bytes 1048592 | tf_op jit(solution)/shard_map/reduce_scatter | solution.py:323
  955.4 25.2 %all-reduce.2 = (f32[1024]{0:T(1024)S(1)}, bf16[2048]{0:T(1024)(128)(2,1)S(1)}, bf16[2048]{0:T(1024)(128)(2,1)S(1)}) all-reduce(f32[1024]{0:T(1024)S(1)} %get-tuple-element.331, f32[2048]{0:T(1024)S(1)} %get-tuple-element.330, f32[2048]{0:T(1024)S(1)} %copy-done.41), channel_id=1, replica_groups=mesh['row'=4,'col'=8] {'col'}, use_global_device_ids=true, to_apply=%region_16.17 | all-reduce | flops 5120 | bytes 32768 | tf_op jit(solution)/shard_map/psum | solution.py:294
  980.6 11.4 %all-reduce.3 = (bf16[2048]{0:T(1024)(128)(2,1)S(1)}, bf16[2048]{0:T(1024)(128)(2,1)S(1)}) all-reduce(bf16[2048]{0:T(1024)(128)(2,1)S(1)} %get-tuple-element.371, bf16[2048]{0:T(1024)(128)(2,1)S(1)} %get-tuple-element.372), channel_id=13, replica_groups=mesh['row'=4,'col'=8] {'row'}, use_global_device_ids=true, to_apply=%region_26.27.clone | all-reduce | flops 4096 | bytes 16384
  995.1 15.6 %reduce-scatter.22.cloned.1.call-done = bf16[512,256]{1,0:T(8,128)(2,1)} async-done(((bf16[2048,256]{1,0:T(8,128)(2,1)}), bf16[512,256]{1,0:T(8,128)(2,1)}) %reduce-scatter.22.cloned.1.call-update) | async-done | bytes 262160 | tf_op jit(solution)/shard_map/reduce_scatter | solution.py:308
  1012.5 26.3 %reduce-scatter.24.cloned.1.call-done = bf16[512,256]{1,0:T(8,128)(2,1)} async-done(((bf16[2048,256]{1,0:T(8,128)(2,1)}), bf16[512,256]{1,0:T(8,128)(2,1)}) %reduce-scatter.24.cloned.1.call-update) | async-done | bytes 262160 | tf_op jit(solution)/shard_map/reduce_scatter | solution.py:311
  1040.6 26.3 %reduce-scatter.26.cloned.1.call-done = bf16[512,256]{1,0:T(8,128)(2,1)} async-done(((bf16[2048,256]{1,0:T(8,128)(2,1)}), bf16[512,256]{1,0:T(8,128)(2,1)}) %reduce-scatter.26.cloned.1.call-update) | async-done | bytes 262160 | tf_op jit(solution)/shard_map/reduce_scatter | solution.py:314
  1068.7 51.6 %reduce-scatter.18.cloned.1.call-done = bf16[1024,256]{1,0:T(8,128)(2,1)} async-done(((bf16[1024,2048]{1,0:T(8,128)(2,1)}), bf16[1024,256]{1,0:T(8,128)(2,1)}) %reduce-scatter.18.cloned.1.call-update) | async-done | bytes 524304 | tf_op jit(solution)/shard_map/reduce_scatter | solution.py:295
  (292 shorter events, 276.2 us)
Async XLA Ops:
  7.2 42.9 %all-gather.13.cloned.1.call-start = ((), (), s32[]{:S(2)}) async-start(), calls=%async_computation.11 | async-start | bytes 4718592 | tf_op jit(solution)/shard_map/all_gather | solution.py:198
  7.9 71.7 %all-gather.17.cloned.1.call-start = ((), (), s32[]{:S(2)}) async-start(), calls=%async_computation.13 | async-start | bytes 1310720 | tf_op jit(solution)/shard_map/all_gather | solution.py:174
  8.7 100.0 %all-gather.15.cloned.1.call-start = ((), (), s32[]{:S(2)}) async-start(), calls=%async_computation.12 | async-start | bytes 1310720 | tf_op jit(solution)/shard_map/all_gather | solution.py:173
  9.4 128.1 %all-gather.19.cloned.1.call-start = ((), (), s32[]{:S(2)}) async-start(), calls=%async_computation.14 | async-start | bytes 1310720 | tf_op jit(solution)/shard_map/all_gather | solution.py:175
  10.0 156.4 %all-gather.21.cloned.1.call-start = ((), (), s32[]{:S(2)}) async-start(), calls=%async_computation.15 | async-start | bytes 1310720 | tf_op jit(solution)/shard_map/all_gather | solution.py:176
  10.6 232.6 %reduce-scatter.12.cloned.1.call-start = ((), (), s32[]{:S(2)}) async-start(), calls=%async_computation.16 | async-start | bytes 9437184 | tf_op jit(solution)/shard_map/reduce_scatter | solution.py:219
  172.3 172.0 %all-gather.27.cloned.1.call-start = ((), (), s32[]{:S(2)}) async-start(), calls=%async_computation.19 | async-start | bytes 5242880 | tf_op jit(solution)/shard_map/all_gather | solution.py:179
  173.0 199.8 %all-gather.29.cloned.1.call-start = ((), (), s32[]{:S(2)}) async-start(), calls=%async_computation.21 | async-start | bytes 4718592 | tf_op jit(solution)/shard_map/all_gather | solution.py:240
  173.8 280.6 %all-gather.25.cloned.1.call-start = ((), (), s32[]{:S(2)}) async-start(), calls=%async_computation.18 | async-start | bytes 5242880 | tf_op jit(solution)/shard_map/all_gather | solution.py:178
  174.5 360.7 %all-gather.23.cloned.1.call-start = ((), (), s32[]{:S(2)}) async-start(), calls=%async_computation.17 | async-start | bytes 5242880 | tf_op jit(solution)/shard_map/all_gather | solution.py:177
  244.5 15.2 %collective-permute-start = (f32[1024,256]{1,0:T(8,128)S(1)}, f32[1024,256]{1,0:T(8,128)S(1)}, u32[]{:S(2)}, u32[]{:S(2)}) collective-permute-start(f32[1024,256]{1,0:T(8,128)S(1)} %convert_add_fusion), channel_id=1, source_target_pairs={{0,1},{1,2},{2,3},{3,4},{4,5},{5,6},{6,7},{7,0},{8,9},{9,10},{10,1... | collective-permute-start | bytes 3145736 | tf_op jit(solution)/shard_map/ppermute | solution.py:223
  260.7 15.1 %collective-permute-start.1 = (f32[1024,256]{1,0:T(8,128)S(1)}, f32[1024,256]{1,0:T(8,128)S(1)}, u32[]{:S(2)}, u32[]{:S(2)}) collective-permute-start(f32[1024,256]{1,0:T(8,128)S(1)} %collective-permute-done), channel_id=1, source_target_pairs={{0,1},{1,2},{2,3},{3,4},{4,5},{5,6},{6,7},{7,0},{8,9},{9,10},{10,1... | collective-permute-start | bytes 3145736 | tf_op jit(solution)/shard_map/ppermute | solution.py:223
  276.8 15.1 %collective-permute-start.2 = (f32[1024,256]{1,0:T(8,128)S(1)}, f32[1024,256]{1,0:T(8,128)S(1)}, u32[]{:S(2)}, u32[]{:S(2)}) collective-permute-start(f32[1024,256]{1,0:T(8,128)S(1)} %collective-permute-done.1), channel_id=1, source_target_pairs={{0,1},{1,2},{2,3},{3,4},{4,5},{5,6},{6,7},{7,0},{8,9},{9,10},{10,1... | collective-permute-start | bytes 3145736 | tf_op jit(solution)/shard_map/ppermute | solution.py:223
  292.9 15.1 %collective-permute-start.3 = (f32[1024,256]{1,0:T(8,128)S(1)}, f32[1024,256]{1,0:T(8,128)S(1)}, u32[]{:S(2)}, u32[]{:S(2)}) collective-permute-start(f32[1024,256]{1,0:T(8,128)S(1)} %collective-permute-done.2), channel_id=1, source_target_pairs={{0,1},{1,2},{2,3},{3,4},{4,5},{5,6},{6,7},{7,0},{8,9},{9,10},{10,1... | collective-permute-start | bytes 3145736 | tf_op jit(solution)/shard_map/ppermute | solution.py:223
  309.0 15.2 %collective-permute-start.4 = (f32[1024,256]{1,0:T(8,128)S(1)}, f32[1024,256]{1,0:T(8,128)}, u32[]{:S(2)}, u32[]{:S(2)}) collective-permute-start(f32[1024,256]{1,0:T(8,128)S(1)} %collective-permute-done.3), channel_id=1, source_target_pairs={{0,1},{1,2},{2,3},{3,4},{4,5},{5,6},{6,7},{7,0},{8,9},{9,10},{10,1... | collective-permute-start | bytes 3145736 | tf_op jit(solution)/shard_map/ppermute | solution.py:223
  324.2 19.8 %collective-permute-start.5 = (f32[1024,256]{1,0:T(8,128)}, f32[1024,256]{1,0:T(8,128)}, u32[]{:S(2)}, u32[]{:S(2)}) collective-permute-start(f32[1024,256]{1,0:T(8,128)} %collective-permute-done.4), channel_id=1, source_target_pairs={{0,1},{1,2},{2,3},{3,4},{4,5},{5,6},{6,7},{7,0},{8,9},{9,10},{10,1... | collective-permute-start | bytes 3145736 | tf_op jit(solution)/shard_map/ppermute | solution.py:223
  324.2 295.7 %reduce-scatter.16.cloned.1.call-start = ((), (), s32[]{:S(2)}) async-start(), calls=%async_computation.22 | async-start | bytes 4718592 | tf_op jit(solution)/shard_map/reduce_scatter | solution.py:253
  344.0 38.7 %collective-permute-start.6 = (f32[1024,256]{1,0:T(8,128)}, f32[1024,256]{1,0:T(8,128)}, u32[]{:S(2)}, u32[]{:S(2)}) collective-permute-start(f32[1024,256]{1,0:T(8,128)} %collective-permute-done.5), channel_id=1, source_target_pairs={{0,1},{1,2},{2,3},{3,4},{4,5},{5,6},{6,7},{7,0},{8,9},{9,10},{10,1... | collective-permute-start | bytes 3145736 | tf_op jit(solution)/shard_map/ppermute | solution.py:223
  569.9 91.0 %all-gather.31.cloned.1.call-start = ((), (), s32[]{:S(2)}) async-start(), calls=%async_computation.23 | async-start | bytes 4718592 | tf_op jit(solution)/shard_map/all_gather | solution.py:260
  622.4 155.3 %reduce-scatter.14.cloned.1.call-start = ((), (), s32[]{:S(2)}) async-start(), calls=%async_computation.20 | async-start | bytes 4718592 | tf_op jit(solution)/shard_map/reduce_scatter | solution.py:236
  632.0 161.9 %reduce-scatter.28.cloned.1.call-start = ((), (), s32[]{:S(2)}) async-start(), calls=%async_computation.29 | async-start | bytes 5242880 | tf_op jit(solution)/shard_map/reduce_scatter | solution.py:317
  641.6 231.6 %reduce-scatter.30.cloned.1.call-start = ((), (), s32[]{:S(2)}) async-start(), calls=%async_computation.30 | async-start | bytes 5242880 | tf_op jit(solution)/shard_map/reduce_scatter | solution.py:320
  651.2 301.6 %reduce-scatter.32.cloned.1.call-start = ((), (), s32[]{:S(2)}) async-start(), calls=%async_computation.31 | async-start | bytes 5242880 | tf_op jit(solution)/shard_map/reduce_scatter | solution.py:323
  660.8 332.5 %reduce-scatter.20.cloned.1.call-start = ((), (), s32[]{:S(2)}) async-start(), calls=%async_computation.25 | async-start | bytes 1310720 | tf_op jit(solution)/shard_map/reduce_scatter | solution.py:305
  747.7 263.0 %reduce-scatter.22.cloned.1.call-start = ((), (), s32[]{:S(2)}) async-start(), calls=%async_computation.26 | async-start | bytes 1310720 | tf_op jit(solution)/shard_map/reduce_scatter | solution.py:308
  752.6 286.3 %reduce-scatter.24.cloned.1.call-start = ((), (), s32[]{:S(2)}) async-start(), calls=%async_computation.27 | async-start | bytes 1310720 | tf_op jit(solution)/shard_map/reduce_scatter | solution.py:311
  758.5 308.4 %reduce-scatter.26.cloned.1.call-start = ((), (), s32[]{:S(2)}) async-start(), calls=%async_computation.28 | async-start | bytes 1310720 | tf_op jit(solution)/shard_map/reduce_scatter | solution.py:314
  763.2 357.1 %reduce-scatter.18.cloned.1.call-start = ((), (), s32[]{:S(2)}) async-start(), calls=%async_computation.24 | async-start | bytes 4718592 | tf_op jit(solution)/shard_map/reduce_scatter | solution.py:295
  796.6 323.7 %copy-start.21 = (bf16[1024,256]{1,0:T(8,128)(2,1)S(1)}, bf16[1024,256]{1,0:T(8,128)(2,1)}, u32[]{:S(2)}) copy-start(bf16[1024,256]{1,0:T(8,128)(2,1)} %reduce-scatter.16.cloned.1.call-done) | copy-start | bytes 1572868
  796.6 323.7 %copy-start.36 = (f32[1024]{0:T(1024)S(1)}, f32[1024]{0:T(1024)}, u32[]{:S(2)}) copy-start(f32[1024]{0:T(1024)} %copy-done.35) | copy-start | bytes 12292
  796.6 323.7 %copy-start.38 = (f32[1024]{0:T(1024)S(1)}, f32[1024]{0:T(1024)}, u32[]{:S(2)}) copy-start(f32[1024]{0:T(1024)} %copy-done.37) | copy-start | bytes 12292
  796.6 323.7 %copy-start.40 = (f32[256]{0:T(256)S(1)}, f32[256]{0:T(256)}, u32[]{:S(2)}) copy-start(f32[256]{0:T(256)} %copy-done.39) | copy-start | bytes 3076
  (50 other events, 1778.0 us)
Sparse Core Ops, SparseCore 0:
  9.9 40.1 all-gather.12
  51.6 27.9 all-gather.16
  81.2 27.4 all-gather.14
  110.0 27.4 all-gather.18
  138.9 27.4 all-gather.20
  172.4 70.7 reduce-scatter.11
  244.8 80.7 all-gather.26
  327.6 45.1 all-gather.28
  374.5 79.8 all-gather.24
  455.8 79.2 all-gather.22
  570.0 49.8 reduce-scatter.15
  622.6 37.4 all-gather.30
  663.4 51.3 reduce-scatter.13
  717.0 76.7 reduce-scatter.27
  796.0 77.2 reduce-scatter.29
  875.5 77.2 reduce-scatter.31
  954.9 27.6 reduce-scatter.19
  984.9 25.8 reduce-scatter.21
  1013.0 25.7 reduce-scatter.23
  1041.1 25.7 reduce-scatter.25
  1070.3 49.9 reduce-scatter.17
